TPU v7x, 512 devices: a whole 4x4x16 slice. The times are simulated.
512 devices in a mesh: grp: 8 (over x, core), seq: 16 (over z_hi, y), head: 4 (over z_lo).
Axes of the slice: x: 4, y: 4, z: 16 (z_hi: 4, z_lo: 4; z = z_hi * 4 + z_lo), core: 2. Of those that a mesh axis runs over, the one named last changes fastest.
Arguments:
- prompt_q: bfloat16 [14336, 8192], P(('grp', 'seq'), 'head'), parts along dimension 0, may hold values from -24 to 24
- prompt_k: bfloat16 [14336, 1024], P(('grp', 'seq'), 'head'), parts along dimension 0, may hold values from -24 to 24
- prompt_v: bfloat16 [14336, 1024], P(('grp', 'seq'), 'head'), parts along dimension 0, may hold values from -6 to 6
- resp_q: bfloat16 [128, 64, 8192], P(('grp', 'seq'), 'head'), parts along dimension 0, may hold values from -24 to 24
- resp_k: bfloat16 [128, 64, 1024], P(('grp', 'seq'), 'head'), parts along dimension 0, may hold values from -24 to 24
- resp_v: bfloat16 [128, 64, 1024], P(('grp', 'seq'), 'head'), parts along dimension 0, may hold values from -6 to 6
- lengths: int32 [128], P(('grp', 'seq')), parts along dimension 0, may hold values from 16 to 64, as said below
Outputs:
- prompt_out: bfloat16 [14336, 8192], P(('grp', 'seq'), 'head'), parts along dimension 0
- resp_out: bfloat16 [128, 64, 8192], P(('grp', 'seq'), 'head'), parts along dimension 0
There are 8 independent parts, one for each index of `grp`. A program takes and returns all parts, laid end to end along the dimension named above; each array names one. Nothing has to cross between parts.
Inputs may be any that keep to these rules, and one draw needn't show every extreme that they name: `lengths`: in every draw one response has exactly 64 tokens and another exactly 16.
All inputs are finite; a program needn't handle non-finite values.
Results may differ from a plain program's by a relative error of at most 0.0075.
Values may be sent and summed in bfloat16 or wider, within the bound.
A program may use at most 64 MiB of HBM per device.

v0:
```python
import math

import jax
import jax.numpy as jnp
from jax import lax
from jax.sharding import PartitionSpec as P

HEAD_DIM = 128
GROUP = 8


very_low = -1e30
key_block = 512


def empty_state(local_kv, row_count):
    return (
        jnp.full((local_kv, GROUP, row_count), very_low, jnp.float32),
        jnp.zeros((local_kv, GROUP, row_count), jnp.float32),
        jnp.zeros((local_kv, GROUP, row_count, HEAD_DIM), jnp.float32),
    )


def blend_in(running, scores, visible, product):
    top_old, total_old, accum_old = running
    masked = jnp.where(visible, scores, very_low)
    top_new = jnp.maximum(top_old, jnp.max(masked, axis=-1))
    weights = jnp.where(visible, jnp.exp(masked - top_new[..., None]), 0.0)
    factor = jnp.exp(top_old - top_new)
    total_new = total_old * factor + jnp.sum(weights, axis=-1)
    accum_new = accum_old * factor[..., None] + product(weights.astype(jnp.bfloat16))
    return (top_new, total_new, accum_new)


def absorb(running, queries, keys_piece, values_piece, key_pos, query_pos):
    key_count = keys_piece.shape[0]
    local_kv = queries.shape[1]
    keys_piece = keys_piece.reshape(key_count, local_kv, HEAD_DIM)
    values_piece = values_piece.reshape(key_count, local_kv, HEAD_DIM)
    for begin in range(0, key_count, key_block):
        finish = min(begin + key_block, key_count)
        keys_part = keys_piece[begin:finish]
        values_part = values_piece[begin:finish]
        scores = jnp.einsum(
            "qxgd,nxd->xgqn", queries, keys_part, preferred_element_type=jnp.float32
        ) / math.sqrt(HEAD_DIM)
        if query_pos is None:
            visible = True
        else:
            visible = key_pos[begin:finish][None, :] <= query_pos[:, None]

        def product(weights, values_part=values_part):
            return jnp.einsum(
                "xgqn,nxd->xgqd", weights, values_part, preferred_element_type=jnp.float32
            )

        running = blend_in(running, scores, visible, product)
    return running


def on_device(prompt_q, prompt_k, prompt_v, resp_q, resp_k, resp_v, lengths):
    local_kv = prompt_k.shape[1] // HEAD_DIM
    prompt_rows = prompt_q.shape[0]
    resp_count = resp_q.shape[0]
    token_rows = resp_q.shape[1]
    head_parts = lax.axis_size("head")
    query_width = resp_q.shape[2] // head_parts
    key_width = resp_k.shape[2] // head_parts
    moved_q, moved_k, moved_v = (
        lax.all_to_all(
            resp_q.reshape(resp_count, token_rows, head_parts, query_width),
            "head",
            split_axis=2,
            concat_axis=1,
            tiled=True,
        ),
        lax.all_to_all(
            resp_k.reshape(resp_count, token_rows, head_parts, key_width),
            "head",
            split_axis=2,
            concat_axis=1,
            tiled=True,
        ),
        lax.all_to_all(
            resp_v.reshape(resp_count, token_rows, head_parts, key_width),
            "head",
            split_axis=2,
            concat_axis=1,
            tiled=True,
        ),
    )
    full_len = moved_q.shape[1]
    resp_queries = moved_q.reshape(resp_count * full_len, local_kv, GROUP, HEAD_DIM)
    prompt_queries = prompt_q.reshape(prompt_rows, local_kv, GROUP, HEAD_DIM)
    query_pos = lax.axis_index("seq") * prompt_rows + jnp.arange(prompt_rows)
    pieces = (
        lax.all_gather(prompt_k, "seq", axis=0, tiled=True),
        lax.all_gather(prompt_v, "seq", axis=0, tiled=True),
    )
    key_pos = jnp.arange(pieces[0].shape[0])
    prompt_state = absorb(
        empty_state(local_kv, prompt_rows), prompt_queries, pieces[0], pieces[1], key_pos, query_pos
    )
    pieces = (
        lax.all_gather(prompt_k, "seq", axis=0, tiled=True),
        lax.all_gather(prompt_v, "seq", axis=0, tiled=True),
    )
    prefix_state = absorb(
        empty_state(local_kv, resp_count * full_len), resp_queries, pieces[0], pieces[1], None, None
    )
    own_q = moved_q.reshape(resp_count, full_len, local_kv, GROUP, HEAD_DIM)
    own_k = moved_k.reshape(resp_count, full_len, local_kv, HEAD_DIM)
    own_v = moved_v.reshape(resp_count, full_len, local_kv, HEAD_DIM)
    own_scores = jnp.einsum(
        "rqxgd,rkxd->xgrqk", own_q, own_k, preferred_element_type=jnp.float32
    ) / math.sqrt(HEAD_DIM)
    positions = jnp.arange(full_len)
    causal = positions[None, :] <= positions[:, None]
    reshaped = (
        prefix_state[0].reshape(local_kv, GROUP, resp_count, full_len),
        prefix_state[1].reshape(local_kv, GROUP, resp_count, full_len),
        prefix_state[2].reshape(local_kv, GROUP, resp_count, full_len, HEAD_DIM),
    )

    def own_product(weights):
        return jnp.einsum("xgrqk,rkxd->xgrqd", weights, own_v, preferred_element_type=jnp.float32)

    merged = blend_in(reshaped, own_scores, causal, own_product)
    result = merged[2] / merged[1][..., None]
    live_rows = positions[None, :] < lengths[:, None]
    result = jnp.where(live_rows[None, None, :, :, None], result, 0.0)
    answer = (
        result.transpose(2, 3, 0, 1, 4)
        .reshape(resp_count, full_len, 1, local_kv * GROUP * HEAD_DIM)
        .astype(jnp.bfloat16)
    )
    returned = lax.all_to_all(answer, "head", split_axis=1, concat_axis=2, tiled=True)
    resp_out = returned.reshape(resp_count, token_rows, head_parts * local_kv * GROUP * HEAD_DIM)
    prompt_result = prompt_state[2] / prompt_state[1][..., None]
    prompt_out = (
        prompt_result.transpose(2, 0, 1, 3)
        .reshape(prompt_rows, local_kv * GROUP * HEAD_DIM)
        .astype(jnp.bfloat16)
    )
    return (prompt_out, resp_out)


def solution(mesh):
    placed = (
        P(("grp", "seq"), "head"),
        P(("grp", "seq"), "head"),
        P(("grp", "seq"), "head"),
        P(("grp", "seq"), "head", None),
        P(("grp", "seq"), "head", None),
        P(("grp", "seq"), "head", None),
        P(("grp", "seq")),
    )
    return jax.shard_map(
        on_device,
        mesh=mesh,
        in_specs=placed,
        out_specs=(P(("grp", "seq"), "head"), P(("grp", "seq"), "head", None)),
        check_vma=False,
    )
```

profile of v0, /device:TPU:24, one launch (start us, length us, event | category | flops | bytes accessed | tf_op | source)
XLA Modules:
  0.0 198.6 jit_solution(12771100201022990043)
XLA Ops:
  0.6 1.4 copy.287
  2.0 5.9 %all-to-all-start.1 = ((bf16[1,16,4,256]{3,1,0,2:T(8,128)(2,1)}), bf16[1,16,4,256]{3,1,0,2:T(8,128)(2,1)}, u32[]{:S(2)}, u32[]{:S(2)}) async-start(bf16[1,16,4,256]{3,1,0,2:T(8,128)(2,1)} %bitcast.332), calls=%async_computation.1 | async-start | bytes 65536 | tf_op jit(solution)/shard_map/all_to_all | solution.py:77
  7.9 64.8 %all_gather.8 = bf16[1792,256]{1,0:T(8,128)(2,1)S(1)} all-gather(bf16[112,256]{1,0:T(8,128)(2,1)} %param.8), channel_id=1, replica_groups=mesh['grp'=8,'seq'=16,'head'=4] {'seq'}, dimensions={0}, use_global_device_ids=true | all-gather | bytes 974848 | tf_op jit(solution)/shard_map/all_gather | solution.py:97
  72.8 66.7 %all_gather.9 = bf16[1792,256]{1,0:T(8,128)(2,1)S(1)} all-gather(bf16[112,256]{1,0:T(8,128)(2,1)S(1)} %copy-done.14), channel_id=1, replica_groups=mesh['grp'=8,'seq'=16,'head'=4] {'seq'}, dimensions={0}, use_global_device_ids=true | all-gather | bytes 974848 | tf_op jit(solution)/shard_map/all_gather | solution.py:98
  141.6 1.1 copy.235
  143.3 0.8 copy.229
  144.2 0.7 copy.231
  145.1 0.8 copy.225
  146.8 0.8 fusion.2
  147.6 0.8 fusion.1
  148.3 0.8 fusion
  149.2 0.8 fusion.58
  150.0 1.2 fusion.7
  151.7 2.3 %fusion.3 = (f32[2,8,112]{2,1,0:T(8,128)S(1)}, f32[2,8,112]{2,1,0:T(8,128)S(1)}) fusion(f32[2,512,112,8]{1,2,3,0:T(8,128)S(1)} %get-tuple-element.38, f32[2,8,112]{2,1,0:T(8,128)S(1)} %get-tuple-element.27, pred[112,512]{1,0:T(8,128)(4,1)S(1)} %get-tuple-element.30, f32[2,8,112]{2,1,0:T(8,128)S(1)} %get-tuple-element.16, ...), kind=kLoop, calls=%fused_computation.9 | loop fusion | flops 9171456 | bytes 7483392 | tf_op jit(solution)/shard_map/reduce_sum | solution.py:30
  154.1 3.3 %all-to-all-start.2 = ((bf16[1,16,4,256]{3,1,0,2:T(8,128)(2,1)}), bf16[1,16,4,256]{3,1,0,2:T(8,128)(2,1)S(1)}, u32[]{:S(2)}, u32[]{:S(2)}) async-start(bf16[1,16,4,256]{3,1,0,2:T(8,128)(2,1)} %bitcast.331), calls=%async_computation.2 | async-start | bytes 65536 | tf_op jit(solution)/shard_map/all_to_all | solution.py:84
  157.4 5.6 %all-to-all-done.2 = bf16[1,16,4,256]{3,1,0,2:T(8,128)(2,1)S(1)} async-done(((bf16[1,16,4,256]{3,1,0,2:T(8,128)(2,1)}), bf16[1,16,4,256]{3,1,0,2:T(8,128)(2,1)S(1)}, u32[]{:S(2)}, u32[]{:S(2)}) %all-to-all-start.2) | async-done | bytes 32800 | tf_op jit(solution)/shard_map/all_to_all | solution.py:84
  163.0 3.6 %all-to-all-start = ((bf16[1,16,4,2048]{3,1,0,2:T(8,128)(2,1)}), bf16[1,16,4,2048]{3,1,0,2:T(8,128)(2,1)S(1)}, u32[]{:S(2)}, u32[]{:S(2)}) async-start(bf16[1,16,4,2048]{3,1,0,2:T(8,128)(2,1)} %bitcast.330), calls=%async_computation | async-start | bytes 524288 | tf_op jit(solution)/shard_map/all_to_all | solution.py:70
  166.6 3.5 %fusion.55 = f32[112,2,8,128]{3,0,2,1:T(8,128)S(1)} fusion(bf16[512,2,128,1]{0,2,3,1:T(8,128)(2,1)} %bitcast.358, f32[2,512,112,8]{1,2,3,0:T(8,128)} %copy-done.2, f32[2,8,112]{2,1,0:T(8,128)S(1)} %get-tuple-element.27, pred[112,512]{1,0:T(8,128)(4,1)} %copy-done.10, f32[112,2,8]{0,2,1:T(8,128)S(1)} %get-tuple-element.23, ...), kind=kOutput, calls=%fused_computation.52 | convolution fusion | flops 239927296 | bytes 4928512 | tf_op jit(solution)/shard_map/xgqn,nxd->xgqd/dot_general | solution.py:53
  170.1 2.5 %fusion.49 = f32[112,2,8,128]{3,0,2,1:T(8,128)} fusion(f32[112,2,8,128]{3,0,2,1:T(8,128)S(1)} %fusion.55, bf16[512,2,128,1]{0,2,3,1:T(8,128)(2,1)S(1)} %bitcast.356, f32[2,512,112,8]{1,2,3,0:T(8,128)S(1)} %copy-done.1, f32[2,8,112]{2,1,0:T(8,128)S(1)} %get-tuple-element.16, pred[112,512]{1,0:T(8,128)(4,1)S(1)} %copy-done.9, ...), kind=kOutput, calls=%fused_computation.50 | convolution fusion | flops 239927296 | bytes 5838848 | tf_op jit(solution)/shard_map/xgqn,nxd->xgqd/dot_general | solution.py:53
  172.6 0.8 reshape.330
  177.3 1.3 fusion.21
  178.7 0.8 fusion.61
  179.5 0.8 fusion.62
  180.4 0.8 fusion.67
  182.4 2.2 %reduce.2 = bf16[64,2048]{1,0:T(8,128)(2,1)S(1)} reduce(bf16[64,1,1,2048]{3,2,1,0:T(2,128)(2,1)S(1)} %bitcast.350, bf16[]{:T(256)} %broadcast.218), dimensions={1,2}, to_apply=%bitcast.304.reduce_sub_computation | reduce | bytes 524290
  184.6 0.9 reshape.353
  185.5 4.8 %all-to-all-start.3 = ((bf16[4,2,16384]{2,1,0:T(2,128)(2,1)}), bf16[4,2,16384]{2,1,0:T(2,128)(2,1)S(1)}, u32[]{:S(2)}, u32[]{:S(2)}) async-start(bf16[4,2,16384]{2,1,0:T(2,128)(2,1)} %reshape.353), calls=%async_computation.3 | async-start | bytes 524288 | tf_op jit(solution)/shard_map/all_to_all | solution.py:137
  190.3 3.5 %fusion.43 = f32[112,2,8,128]{3,0,2,1:T(8,128)S(1)} fusion(f32[112,2,8,128]{3,0,2,1:T(8,128)} %fusion.49, bf16[512,2,128,1]{0,2,3,1:T(8,128)(2,1)S(1)} %bitcast.361, f32[2,512,112,8]{1,2,3,0:T(8,128)} %copy-done.3, f32[2,8,112]{2,1,0:T(8,128)S(1)} %get-tuple-element.15, pred[112,512]{1,0:T(8,128)(4,1)S(1)} %get-tuple-element.28, ...), kind=kOutput, calls=%fused_computation.48 | convolution fusion | flops 239927296 | bytes 5838848 | tf_op jit(solution)/shard_map/xgqn,nxd->xgqd/dot_general | solution.py:53
  193.8 0.9 fusion.60
  194.9 0.9 copy.284
  195.8 1.3 all-to-all-done.3
  197.7 0.9 reshape.334
  (79 shorter events, 9.5 us)
Async XLA Ops:
  0.6 72.2 %copy-start.14 = (bf16[112,256]{1,0:T(8,128)(2,1)S(1)}, bf16[112,256]{1,0:T(8,128)(2,1)}, u32[]{:S(2)}) copy-start(bf16[112,256]{1,0:T(8,128)(2,1)} %param.9) | copy-start | bytes 172036
  2.0 152.1 %all-to-all-start.1 = ((bf16[1,16,4,256]{3,1,0,2:T(8,128)(2,1)}), bf16[1,16,4,256]{3,1,0,2:T(8,128)(2,1)}, u32[]{:S(2)}, u32[]{:S(2)}) async-start(bf16[1,16,4,256]{3,1,0,2:T(8,128)(2,1)} %bitcast.332), calls=%async_computation.1 | async-start | bytes 65536 | tf_op jit(solution)/shard_map/all_to_all | solution.py:77
  72.8 66.8 %copy-start.4 = (bf16[1792,256]{1,0:T(8,128)(2,1)}, bf16[1792,256]{1,0:T(8,128)(2,1)S(1)}, u32[]{:S(2)}) copy-start(bf16[1792,256]{1,0:T(8,128)(2,1)S(1)} %all_gather.8) | copy-start | bytes 2752516
  72.8 67.5 %copy-start.15 = (bf16[1,16,1024]{2,1,0:T(8,128)(2,1)S(1)}, bf16[1,16,1024]{2,1,0:T(8,128)(2,1)}, u32[]{:S(2)}) copy-start(bf16[1,16,1024]{2,1,0:T(8,128)(2,1)} %param.12) | copy-start | bytes 98308
  72.8 68.1 %copy-start.11 = (bf16[1,16,8192]{2,1,0:T(8,128)(2,1)S(1)}, bf16[1,16,8192]{2,1,0:T(8,128)(2,1)}, u32[]{:S(2)}) copy-start(bf16[1,16,8192]{2,1,0:T(8,128)(2,1)} %param.10) | copy-start | bytes 786436
  139.6 3.3 %slice-start = ((bf16[1792,256]{1,0:T(8,128)(2,1)}), bf16[256,256]{1,0:T(8,128)(2,1)S(1)}, s32[]{:S(2)}) async-start(bf16[1792,256]{1,0:T(8,128)(2,1)} %copy-done.4), calls=%async_computation.4 | async-start | bytes 262144 | tf_op jit(solution)/shard_map/slice | solution.py:42
  146.0 3.2 %copy-start.12 = (pred[112,256]{1,0:T(8,128)(4,1)}, pred[112,256]{1,0:T(8,128)(4,1)S(1)}, u32[]{:S(2)}) copy-start(pred[112,256]{1,0:T(8,128)(4,1)S(1)} %broadcast_compare_fusion.3) | copy-start | bytes 86020
  146.2 5.0 %copy-start.8 = (pred[112,512]{1,0:T(8,128)(4,1)}, pred[112,512]{1,0:T(8,128)(4,1)S(1)}, u32[]{:S(2)}) copy-start(pred[112,512]{1,0:T(8,128)(4,1)S(1)} %get-tuple-element.29) | copy-start | bytes 172036
  146.2 5.0 %copy-start.10 = (pred[112,512]{1,0:T(8,128)(4,1)}, pred[112,512]{1,0:T(8,128)(4,1)S(1)}, u32[]{:S(2)}) copy-start(pred[112,512]{1,0:T(8,128)(4,1)S(1)} %get-tuple-element.30) | copy-start | bytes 172036
  147.5 2.4 %copy-start.3 = (f32[2,512,112,8]{1,2,3,0:T(8,128)}, f32[2,512,112,8]{1,2,3,0:T(8,128)S(1)}, u32[]{:S(2)}) copy-start(f32[2,512,112,8]{1,2,3,0:T(8,128)S(1)} %get-tuple-element.34) | copy-start | bytes 11010052
  148.3 2.9 %copy-start = (f32[2,512,112,8]{1,2,3,0:T(8,128)}, f32[2,512,112,8]{1,2,3,0:T(8,128)S(1)}, u32[]{:S(2)}) copy-start(f32[2,512,112,8]{1,2,3,0:T(8,128)S(1)} %get-tuple-element.36) | copy-start | bytes 11010052
  149.1 2.6 %copy-start.2 = (f32[2,512,112,8]{1,2,3,0:T(8,128)}, f32[2,512,112,8]{1,2,3,0:T(8,128)S(1)}, u32[]{:S(2)}) copy-start(f32[2,512,112,8]{1,2,3,0:T(8,128)S(1)} %get-tuple-element.38) | copy-start | bytes 11010052
  154.1 8.9 %all-to-all-start.2 = ((bf16[1,16,4,256]{3,1,0,2:T(8,128)(2,1)}), bf16[1,16,4,256]{3,1,0,2:T(8,128)(2,1)S(1)}, u32[]{:S(2)}, u32[]{:S(2)}) async-start(bf16[1,16,4,256]{3,1,0,2:T(8,128)(2,1)} %bitcast.331), calls=%async_computation.2 | async-start | bytes 65536 | tf_op jit(solution)/shard_map/all_to_all | solution.py:84
  163.0 10.4 %all-to-all-start = ((bf16[1,16,4,2048]{3,1,0,2:T(8,128)(2,1)}), bf16[1,16,4,2048]{3,1,0,2:T(8,128)(2,1)S(1)}, u32[]{:S(2)}, u32[]{:S(2)}) async-start(bf16[1,16,4,2048]{3,1,0,2:T(8,128)(2,1)} %bitcast.330), calls=%async_computation | async-start | bytes 524288 | tf_op jit(solution)/shard_map/all_to_all | solution.py:70
  166.6 3.5 %copy-start.1 = (f32[2,512,112,8]{1,2,3,0:T(8,128)S(1)}, f32[2,512,112,8]{1,2,3,0:T(8,128)}, u32[]{:S(2)}) copy-start(f32[2,512,112,8]{1,2,3,0:T(8,128)} %copy-done) | copy-start | bytes 11010052
  166.6 3.5 %copy-start.9 = (pred[112,512]{1,0:T(8,128)(4,1)S(1)}, pred[112,512]{1,0:T(8,128)(4,1)}, u32[]{:S(2)}) copy-start(pred[112,512]{1,0:T(8,128)(4,1)} %copy-done.8) | copy-start | bytes 172036
  174.9 1.3 copy-start.7
  177.3 1.4 copy-start.5
  179.5 1.0 copy-start.6
  185.5 11.6 %all-to-all-start.3 = ((bf16[4,2,16384]{2,1,0:T(2,128)(2,1)}), bf16[4,2,16384]{2,1,0:T(2,128)(2,1)S(1)}, u32[]{:S(2)}, u32[]{:S(2)}) async-start(bf16[4,2,16384]{2,1,0:T(2,128)(2,1)} %reshape.353), calls=%async_computation.3 | async-start | bytes 524288 | tf_op jit(solution)/shard_map/all_to_all | solution.py:137
  190.3 3.5 %copy-start.13 = (pred[112,256]{1,0:T(8,128)(4,1)S(1)}, pred[112,256]{1,0:T(8,128)(4,1)}, u32[]{:S(2)}) copy-start(pred[112,256]{1,0:T(8,128)(4,1)} %copy-done.12) | copy-start | bytes 86020
where the time goes:
time: 202 us; the launch traced here: 199 us
  blocking collectives  132 us (65%)
  matrix products  18.7 us (9%)
  starting transfers between devices  17.6 us (9%)
  local copies, waits for them, and re-layouts  12.8 us (6%)
  other arithmetic  9.24 us (5%)
  waiting for transfers between devices  6.91 us (3%)
    all_gather x1, blocking collectives, on_device(): lax.all_gather(prompt_v, 'seq', axis=0, tiled=True)  66.7 us
    all_gather x1, blocking collectives, on_device(): lax.all_gather(prompt_k, 'seq', axis=0, tiled=True)  64.8 us
    dot_general x8, matrix products, product(): jnp.einsum('xgqn,nxd->xgqd', weights, values_part, preferred_element_type...  13.2 us
    unnamed x47, local copies, waits for them, and re-layouts  7.65 us
    reduce_sum x7, other arithmetic, blend_in(): total_new = total_old * factor + jnp.sum(weights, axis=-1)  6.74 us
    all_to_all x1, starting transfers between devices, on_device(): lax.all_to_all(resp_k.reshape(resp_count, token_rows, head_parts, key_wid...  5.89 us
    all_to_all x1, waiting for transfers between devices, on_device(): lax.all_to_all(resp_v.reshape(resp_count, token_rows, head_parts, key_wid...  5.61 us
    all_to_all x1, starting transfers between devices, on_device(): lax.all_to_all(answer, 'head', split_axis=1, concat_axis=2, tiled=True)  4.85 us
  transfers between devices with their start and end apart: 4, of which 2 were waited for; matrix products, arithmetic and copies ran while one was open for 13% of the time, Pallas kernels for 0%

commit v1 on v0

v1 whole, which is shorter than its diff:
```python
import functools
import math

import jax
import jax.numpy as jnp
from jax import lax
from jax.experimental import pallas as pl
from jax.experimental.pallas import tpu as pltpu
from jax.sharding import PartitionSpec as P

HEAD_DIM = 128
GROUP = 8
MESH = pl.DeviceIdType.MESH
SCALE = math.log2(math.e) / math.sqrt(HEAD_DIM)
very_low = -1e30

RING = 4


def kernel(
    sizes,
    pq_ref, pk_ref, pv_ref, rq_ref, rk_ref, rv_ref,
    po_ref, ro_ref,
    kbuf, vbuf, pq, rqb, rkb, rvb, qs, top, acc, pob, rob,
    send_sem, recv_sem, local_sem,
):
    rows, toks, parts = sizes
    kv = 2
    wide = GROUP * HEAD_DIM
    qwidth = kv * wide
    resp_rows = GROUP * parts * toks
    chunk = RING * rows

    seq = lax.axis_index("seq")
    head = lax.axis_index("head")
    zh, y = seq // RING, lax.rem(seq, RING)

    def at(dz, dy):
        return lax.rem(zh + dz + RING, RING) * RING + lax.rem(y + dy + RING, RING)

    z_next, z_prev = at(1, 0), at(-1, 0)
    y_next, y_prev = at(0, 1), at(0, -1)
    others = [lax.rem(head + d, parts) for d in range(1, parts)]

    barrier = pltpu.get_barrier_semaphore()
    for peer in (z_next, z_prev, y_next, y_prev):
        pl.semaphore_signal(barrier, inc=1, device_id={"seq": peer}, device_id_type=MESH)
    for peer in others:
        pl.semaphore_signal(barrier, inc=1, device_id={"head": peer}, device_id_type=MESH)

    def rows_of(dy):
        return pl.ds(pl.multiple_of(lax.rem(y + dy + RING, RING) * rows, 16), rows)

    def cols(x):
        return pl.ds(x * HEAD_DIM, HEAD_DIM)

    mine = rows_of(0)
    bufs, given = {"k": kbuf, "v": vbuf}, {"k": pk_ref, "v": pv_ref}

    local = []

    def bring(src, dst):
        copy = pltpu.make_async_copy(src, dst, local_sem.at[len(local)])
        copy.start()
        local.append(copy)
        return copy

    got_pq = bring(pq_ref, pq)
    got_kv = [bring(given[a], bufs[a].at[0, mine, :]) for a in "kv"]
    own_q = pl.ds(pl.multiple_of(head * qwidth, qwidth), qwidth)
    own_kv = pl.ds(pl.multiple_of(head * kv * HEAD_DIM, kv * HEAD_DIM), kv * HEAD_DIM)
    got_resp = [
        bring(rq_ref.at[:, own_q], rqb.at[head]),
        bring(rk_ref.at[:, own_kv], rkb.at[head]),
        bring(rv_ref.at[:, own_kv], rvb.at[head]),
    ]
    pl.semaphore_wait(barrier, 4 + len(others))

    sent = {}

    def send(name, src, dst, peer):
        copy = pltpu.make_async_remote_copy(
            src_ref=src,
            dst_ref=dst,
            send_sem=send_sem.at[len(sent)],
            recv_sem=recv_sem.at[len(sent)],
            device_id=peer,
            device_id_type=MESH,
        )
        copy.start()
        sent[name] = copy

    def arrived(name):
        sent[name].wait_recv()

    def z1(a, x, way):
        slot = 1 if way > 0 else 2
        send(
            ("z1", a, x, way), given[a].at[:, cols(x)], bufs[a].at[slot, mine, cols(x)],
            {"seq": z_next if way > 0 else z_prev},
        )

    def z2(a, x):
        slot, peer = (1, z_next) if a == "k" else (2, z_prev)
        send(
            ("z2", a, x), bufs[a].at[slot, mine, cols(x)], bufs[a].at[3, mine, cols(x)],
            {"seq": peer},
        )

    def y1(a, x, slot):
        place = bufs[a].at[slot, mine, cols(x)]
        src = given[a].at[:, cols(x)] if slot == 0 else place
        for way in (1, -1) if a == "k" else (-1, 1):
            send(("y1", a, x, slot, way), src, place, {"seq": y_next if way > 0 else y_prev})

    def y2(x, slot):
        for a, way in (("k", 1), ("v", -1)):
            arrived(("y1", a, x, slot, way))
            place = bufs[a].at[slot, rows_of(-way), cols(x)]
            send(("y2", a, x, slot), place, place, {"seq": y_next if way > 0 else y_prev})

    def whole(x, slot):
        for a, way in (("k", -1), ("v", 1)):
            arrived(("y1", a, x, slot, way))
        for a in "kv":
            arrived(("y2", a, x, slot))

    def swap_q(x):
        for d, peer in enumerate(others):
            begin = pl.multiple_of(peer * qwidth + x * wide, wide)
            send(
                ("q", x, d), rq_ref.at[:, pl.ds(begin, wide)],
                rqb.at[head, :, pl.ds(x * wide, wide)], {"head": peer},
            )

    def swap_kv():
        for d, peer in enumerate(others):
            begin = pl.multiple_of(peer * kv * HEAD_DIM, kv * HEAD_DIM)
            for name, src, dst in (("rk", rk_ref, rkb), ("rv", rv_ref, rvb)):
                send(
                    (name, d), src.at[:, pl.ds(begin, kv * HEAD_DIM)], dst.at[head],
                    {"head": peer},
                )

    def swap_out(x):
        to = pl.multiple_of(head * qwidth + x * wide, wide)
        for d, peer in enumerate(others):
            send(
                ("o", x, d), rob.at[peer, :, pl.ds(x * wide, wide)],
                ro_ref.at[:, pl.ds(to, wide)], {"head": peer},
            )
        bring(rob.at[head, :, pl.ds(x * wide, wide)], ro_ref.at[:, pl.ds(to, wide)])

    def attend(x, keys, values, begin, tile, count, first, visible):
        def body(i, carry):
            here = pl.ds(pl.multiple_of(begin + i * tile, 16), tile)
            k, v = keys(), values()
            scores = lax.dot_general(
                qs[x, here, :], k, (((1,), (1,)), ((), ())), preferred_element_type=jnp.float32
            )
            if visible is not None:
                scores = jnp.where(visible(scores.shape), scores, very_low)
            high = jnp.max(scores, axis=1, keepdims=True)
            if first:
                high = jnp.broadcast_to(high, (tile, HEAD_DIM))
            else:
                before = top[x, here, :]
                high = jnp.maximum(before, high)
            top[x, here, :] = high
            count_keys = k.shape[0]
            spread = jnp.concatenate([high] * -(-count_keys // HEAD_DIM), axis=1)[:, :count_keys]
            weights = jnp.exp2((scores - spread) * SCALE).astype(jnp.bfloat16)
            both = jnp.concatenate([v, jnp.ones_like(v)], axis=1)
            mixed = jnp.dot(weights, both, preferred_element_type=jnp.float32)
            if not first:
                factor = jnp.exp2((before - high) * SCALE)
                mixed = acc[x, here, :] * jnp.concatenate([factor, factor], axis=1) + mixed
            acc[x, here, :] = mixed
            return carry

        lax.fori_loop(0, count, body, 0)

    def block(buf, slot, x):
        return lambda: buf[slot, :, x * HEAD_DIM : (x + 1) * HEAD_DIM]

    per = parts * toks
    resp_tile, prompt_tile = 2 * per, rows

    def resp_slot(x, slot):
        attend(
            x, block(kbuf, slot, x), block(vbuf, slot, x), 0, resp_tile, resp_rows // resp_tile,
            False, None,
        )

    def resp_own(x):
        def flat(buf):
            return lambda: buf[:, :, x * HEAD_DIM : (x + 1) * HEAD_DIM].reshape(per, HEAD_DIM)

        def visible(shape):
            row = lax.rem(lax.broadcasted_iota(jnp.int32, shape, 0), per)
            return lax.broadcasted_iota(jnp.int32, shape, 1) <= row

        attend(x, flat(rkb), flat(rvb), 0, resp_tile, resp_rows // resp_tile, True, visible)

    def prompt_slot(x, slot):
        def visible(shape):
            row = lax.broadcasted_iota(jnp.int32, shape, 0) + y * rows
            return lax.broadcasted_iota(jnp.int32, shape, 1) <= row

        def run():
            attend(
                x, block(kbuf, slot, x), block(vbuf, slot, x), resp_rows, prompt_tile, GROUP,
                slot == 0, visible if slot == 0 else None,
            )

        if slot == 0:
            run()
        else:
            pl.when({1: zh >= 1, 2: zh == RING - 1, 3: zh >= 2}[slot])(run)

    def stack_prompt():
        for x in range(kv):
            for g in range(GROUP):
                at_col = (x * GROUP + g) * HEAD_DIM
                qs[x, pl.ds(resp_rows + g * rows, rows), :] = pq[:, at_col : at_col + HEAD_DIM]

    def stack_resp(x):
        for g in range(GROUP):
            at_col = (x * GROUP + g) * HEAD_DIM
            qs[x, pl.ds(g * per, per), :] = rqb[:, :, at_col : at_col + HEAD_DIM].reshape(
                per, HEAD_DIM
            )

    def quotient(x, begin, count):
        part = acc[x, pl.ds(begin, count), :]
        return (part[:, :HEAD_DIM] / part[:, HEAD_DIM:]).astype(jnp.bfloat16)

    def finish_resp(x):
        for g in range(GROUP):
            at_col = (x * GROUP + g) * HEAD_DIM
            rob[:, :, at_col : at_col + HEAD_DIM] = quotient(x, g * per, per).reshape(
                parts, toks, HEAD_DIM
            )

    def finish_prompt(x):
        for g in range(GROUP):
            at_col = (x * GROUP + g) * HEAD_DIM
            pob[:, at_col : at_col + HEAD_DIM] = quotient(x, resp_rows + g * rows, rows)
        part = pl.ds(x * wide, wide)
        bring(pob.at[:, part], po_ref.at[:, part])

    def first_sends(x):
        z1("k", x, 1)
        z1("v", x, -1)
        z1("v", x, 1)
        z1("k", x, -1)
        y1("k", x, 0)
        y1("v", x, 0)

    def after_z1(x):
        arrived(("z1", "k", x, 1))
        z2("k", x)
        y1("k", x, 1)
        arrived(("z1", "v", x, -1))
        z2("v", x)
        y1("v", x, 2)
        arrived(("z1", "v", x, 1))
        y1("v", x, 1)
        arrived(("z1", "k", x, -1))
        y1("k", x, 2)

    def after_z2(x):
        for a in "kv":
            arrived(("z2", a, x))
            y1(a, x, 3)

    def take_resp(x):
        if x == 0:
            for d in range(parts - 1):
                arrived(("rk", d))
                arrived(("rv", d))
        for d in range(parts - 1):
            arrived(("q", x, d))
        stack_resp(x)

    first_sends(0)
    swap_q(0)
    swap_kv()
    first_sends(1)
    swap_q(1)

    got_pq.wait()
    stack_prompt()
    for copy in got_kv + got_resp:
        copy.wait()
    y2(0, 0)
    y2(1, 0)
    whole(0, 0)
    prompt_slot(0, 0)
    after_z1(0)
    whole(1, 0)
    prompt_slot(1, 0)
    after_z1(1)
    y2(0, 1)
    y2(0, 2)
    take_resp(0)
    resp_own(0)
    resp_slot(0, 0)
    after_z2(0)
    y2(1, 1)
    y2(1, 2)
    whole(0, 1)
    resp_slot(0, 1)
    prompt_slot(0, 1)
    after_z2(1)
    y2(0, 3)
    whole(0, 2)
    resp_slot(0, 2)
    prompt_slot(0, 2)
    y2(1, 3)
    whole(0, 3)
    resp_slot(0, 3)
    finish_resp(0)
    swap_out(0)
    take_resp(1)
    resp_own(1)
    resp_slot(1, 0)
    whole(1, 1)
    resp_slot(1, 1)
    whole(1, 2)
    resp_slot(1, 2)
    whole(1, 3)
    resp_slot(1, 3)
    finish_resp(1)
    swap_out(1)
    prompt_slot(0, 3)
    finish_prompt(0)
    prompt_slot(1, 1)
    prompt_slot(1, 2)
    prompt_slot(1, 3)
    finish_prompt(1)
    for x in range(kv):
        for d in range(parts - 1):
            arrived(("o", x, d))
    for copy in sent.values():
        copy.wait_send()
    for copy in local[6:]:
        copy.wait()


def on_device(prompt_q, prompt_k, prompt_v, resp_q, resp_k, resp_v, lengths):
    rows, qwidth = prompt_q.shape
    kwidth = prompt_k.shape[1]
    toks = resp_q.shape[1]
    parts = lax.axis_size("head")
    kv = kwidth // HEAD_DIM
    total = GROUP * (rows + parts * toks)
    any_place = pl.BlockSpec(memory_space=pl.ANY)
    bf16 = jnp.bfloat16
    messages = 80
    prompt_out, mixed = pl.pallas_call(
        functools.partial(kernel, (rows, toks, parts)),
        out_shape=(
            jax.ShapeDtypeStruct((rows, qwidth), bf16),
            jax.ShapeDtypeStruct((toks, parts * qwidth), bf16),
        ),
        in_specs=[any_place] * 6,
        out_specs=(any_place, any_place),
        scratch_shapes=[
            pltpu.VMEM((RING, RING * rows, kwidth), bf16),
            pltpu.VMEM((RING, RING * rows, kwidth), bf16),
            pltpu.VMEM((rows, qwidth), bf16),
            pltpu.VMEM((parts, toks, qwidth), bf16),
            pltpu.VMEM((parts, toks, kwidth), bf16),
            pltpu.VMEM((parts, toks, kwidth), bf16),
            pltpu.VMEM((kv, total, HEAD_DIM), bf16),
            pltpu.VMEM((kv, total, HEAD_DIM), jnp.float32),
            pltpu.VMEM((kv, total, 2 * HEAD_DIM), jnp.float32),
            pltpu.VMEM((rows, qwidth), bf16),
            pltpu.VMEM((parts, toks, qwidth), bf16),
            pltpu.SemaphoreType.DMA((messages,)),
            pltpu.SemaphoreType.DMA((messages,)),
            pltpu.SemaphoreType.DMA((16,)),
        ],
        compiler_params=pltpu.CompilerParams(
            collective_id=0, has_side_effects=True, vmem_limit_bytes=48 * 1024 * 1024
        ),
    )(prompt_q, prompt_k, prompt_v, resp_q[0], resp_k[0], resp_v[0])
    positions = lax.axis_index("head") * toks + jnp.arange(toks)
    live = positions < lengths[0]
    resp_out = jnp.where(live[:, None], mixed, jnp.zeros_like(mixed))[None]
    return (prompt_out, resp_out)


def solution(mesh):
    placed = (
        P(("grp", "seq"), "head"),
        P(("grp", "seq"), "head"),
        P(("grp", "seq"), "head"),
        P(("grp", "seq"), "head", None),
        P(("grp", "seq"), "head", None),
        P(("grp", "seq"), "head", None),
        P(("grp", "seq")),
    )
    return jax.shard_map(
        on_device,
        mesh=mesh,
        in_specs=placed,
        out_specs=(P(("grp", "seq"), "head"), P(("grp", "seq"), "head", None)),
        check_vma=False,
    )
```

time: 202 us -> 77.1 us (0.38)
  the two profiles are of different devices: /device:TPU:24 before, /device:TPU:418 now
where the time goes in v1:
time: 77.1 us; the launch traced here: 76.7 us
  Pallas kernels  68.7 us (89%)
  local copies, waits for them, and re-layouts  5.88 us (8%)
  between operations  1.31 us (2%)
  other arithmetic  0.8 us (1%)
    pallas_call x1, Pallas kernels, on_device(): pl.pallas_call(functools.partial(kernel, (rows, toks, parts)), out_shape=...  68.7 us
    unnamed x13, local copies, waits for them, and re-layouts  5.88 us

profile of v1, /device:TPU:418, one launch (start us, length us, event | category | flops | bytes accessed | tf_op | source)
XLA Modules:
  0.0 76.7 jit_solution(5437585894575842912)
XLA Ops:
  0.6 0.0 copy-start
  0.6 1.0 %copy-done = bf16[112,2048]{1,0:T(8,128)(2,1)S(1)} copy-done((bf16[112,2048]{1,0:T(8,128)(2,1)S(1)}, bf16[112,2048]{1,0:T(8,128)(2,1)}, u32[]{:S(2)}) %copy-start) | copy-done | bytes 458776
  1.7 0.0 copy-start.1
  1.7 0.9 %copy-done.1 = bf16[1,16,8192]{2,1,0:T(8,128)(2,1)S(1)} copy-done((bf16[1,16,8192]{2,1,0:T(8,128)(2,1)S(1)}, bf16[1,16,8192]{2,1,0:T(8,128)(2,1)}, u32[]{:S(2)}) %copy-start.1) | copy-done | bytes 262168
  2.6 0.0 copy-start.2
  2.6 0.8 %copy-done.2 = bf16[112,256]{1,0:T(8,128)(2,1)S(1)} copy-done((bf16[112,256]{1,0:T(8,128)(2,1)S(1)}, bf16[112,256]{1,0:T(8,128)(2,1)}, u32[]{:S(2)}) %copy-start.2) | copy-done | bytes 57368
  3.4 0.0 copy-start.3
  3.4 0.8 %copy-done.3 = bf16[112,256]{1,0:T(8,128)(2,1)S(1)} copy-done((bf16[112,256]{1,0:T(8,128)(2,1)S(1)}, bf16[112,256]{1,0:T(8,128)(2,1)}, u32[]{:S(2)}) %copy-start.3) | copy-done | bytes 57368
  4.2 0.0 copy-start.4
  4.2 0.8 copy-done.4
  5.0 0.0 copy-start.5
  5.0 0.8 copy-done.5
  5.8 68.7 %shard_map.86 = (bf16[112,2048]{1,0:T(8,128)(2,1)S(1)}, bf16[16,8192]{1,0:T(8,128)(2,1)S(1)}) custom-call(bf16[112,2048]{1,0:T(8,128)(2,1)S(1)} %copy-done, bf16[112,256]{1,0:T(8,128)(2,1)S(1)} %copy-done.2, bf16[112,256]{1,0:T(8,128)(2,1)S(1)} %copy-done.3, bf16[16,8192]{1,0:T(8,128)(2,1)S(1)} %bitcast.7, bf16[16,1024]{1,0:T(8,128)(2,1)S(1)} %bitcast.8, ...), custom_call_target="tpu_custom_call" | custom-call | tf_op jit(solution)/shard_map/pallas_call | solution.py:361
  75.1 0.8 %select_bitcast_fusion = bf16[1,16,8192]{2,1,0:T(8,128)(2,1)} fusion(bf16[16,8192]{1,0:T(8,128)(2,1)S(1)} %get-tuple-element.5, pred[16]{0:T(512)(128)(4,1)S(1)} %add_compare_fusion), kind=kLoop, calls=%fused_computation | loop fusion | flops 131072 | bytes 524304 | tf_op jit(solution)/shard_map/broadcast_in_dim | solution.py:391
  75.9 0.8 %copy.11 = bf16[112,2048]{1,0:T(8,128)(2,1)} copy(bf16[112,2048]{1,0:T(8,128)(2,1)S(1)} %get-tuple-element.8) | data formatting | bytes 917504
  (1 shorter events, 0.0 us)
Async XLA Ops:
  0.6 1.0 %copy-start = (bf16[112,2048]{1,0:T(8,128)(2,1)S(1)}, bf16[112,2048]{1,0:T(8,128)(2,1)}, u32[]{:S(2)}) copy-start(bf16[112,2048]{1,0:T(8,128)(2,1)} %pq_ref.1) | copy-start | bytes 1376260
  1.7 0.9 %copy-start.1 = (bf16[1,16,8192]{2,1,0:T(8,128)(2,1)S(1)}, bf16[1,16,8192]{2,1,0:T(8,128)(2,1)}, u32[]{:S(2)}) copy-start(bf16[1,16,8192]{2,1,0:T(8,128)(2,1)} %param.10) | copy-start | bytes 786436
  2.6 0.8 %copy-start.2 = (bf16[112,256]{1,0:T(8,128)(2,1)S(1)}, bf16[112,256]{1,0:T(8,128)(2,1)}, u32[]{:S(2)}) copy-start(bf16[112,256]{1,0:T(8,128)(2,1)} %pk_ref.1) | copy-start | bytes 172036
  3.4 0.8 %copy-start.3 = (bf16[112,256]{1,0:T(8,128)(2,1)S(1)}, bf16[112,256]{1,0:T(8,128)(2,1)}, u32[]{:S(2)}) copy-start(bf16[112,256]{1,0:T(8,128)(2,1)} %pv_ref.1) | copy-start | bytes 172036
  4.2 0.8 copy-start.4
  5.0 0.8 copy-start.5

commit v2 on v1

--- a/solution.py
+++ b/solution.py
@@ -51,9 +51,6 @@
     def rows_of(dy):
         return pl.ds(pl.multiple_of(lax.rem(y + dy + RING, RING) * rows, 16), rows)
 
-    def cols(x):
-        return pl.ds(x * HEAD_DIM, HEAD_DIM)
-
     mine = rows_of(0)
     bufs, given = {"k": kbuf, "v": vbuf}, {"k": pk_ref, "v": pv_ref}
 
@@ -66,7 +63,11 @@
         return copy
 
     got_pq = bring(pq_ref, pq)
-    got_kv = [bring(given[a], bufs[a].at[0, mine, :]) for a in "kv"]
+    got_kv = [
+        bring(given[a].at[:, pl.ds(x * HEAD_DIM, HEAD_DIM)], bufs[a].at[0, x, mine])
+        for x in range(kv)
+        for a in "kv"
+    ]
     own_q = pl.ds(pl.multiple_of(head * qwidth, qwidth), qwidth)
     own_kv = pl.ds(pl.multiple_of(head * kv * HEAD_DIM, kv * HEAD_DIM), kv * HEAD_DIM)
     got_resp = [
@@ -96,27 +97,26 @@
     def z1(a, x, way):
         slot = 1 if way > 0 else 2
         send(
-            ("z1", a, x, way), given[a].at[:, cols(x)], bufs[a].at[slot, mine, cols(x)],
+            ("z1", a, x, way), bufs[a].at[0, x, mine], bufs[a].at[slot, x, mine],
             {"seq": z_next if way > 0 else z_prev},
         )
 
     def z2(a, x):
         slot, peer = (1, z_next) if a == "k" else (2, z_prev)
         send(
-            ("z2", a, x), bufs[a].at[slot, mine, cols(x)], bufs[a].at[3, mine, cols(x)],
+            ("z2", a, x), bufs[a].at[slot, x, mine], bufs[a].at[3, x, mine],
             {"seq": peer},
         )
 
     def y1(a, x, slot):
-        place = bufs[a].at[slot, mine, cols(x)]
-        src = given[a].at[:, cols(x)] if slot == 0 else place
+        place = bufs[a].at[slot, x, mine]
         for way in (1, -1) if a == "k" else (-1, 1):
-            send(("y1", a, x, slot, way), src, place, {"seq": y_next if way > 0 else y_prev})
+            send(("y1", a, x, slot, way), place, place, {"seq": y_next if way > 0 else y_prev})
 
     def y2(x, slot):
         for a, way in (("k", 1), ("v", -1)):
             arrived(("y1", a, x, slot, way))
-            place = bufs[a].at[slot, rows_of(-way), cols(x)]
+            place = bufs[a].at[slot, x, rows_of(-way)]
             send(("y2", a, x, slot), place, place, {"seq": y_next if way > 0 else y_prev})
 
     def whole(x, slot):
@@ -152,8 +152,8 @@
         bring(rob.at[head, :, pl.ds(x * wide, wide)], ro_ref.at[:, pl.ds(to, wide)])
 
     def attend(x, keys, values, begin, tile, count, first, visible):
-        def body(i, carry):
-            here = pl.ds(pl.multiple_of(begin + i * tile, 16), tile)
+        for i in range(count):
+            here = pl.ds(begin + i * tile, tile)
             k, v = keys(), values()
             scores = lax.dot_general(
                 qs[x, here, :], k, (((1,), (1,)), ((), ())), preferred_element_type=jnp.float32
@@ -176,15 +176,12 @@
                 factor = jnp.exp2((before - high) * SCALE)
                 mixed = acc[x, here, :] * jnp.concatenate([factor, factor], axis=1) + mixed
             acc[x, here, :] = mixed
-            return carry
-
-        lax.fori_loop(0, count, body, 0)
 
     def block(buf, slot, x):
-        return lambda: buf[slot, :, x * HEAD_DIM : (x + 1) * HEAD_DIM]
+        return lambda: buf[slot, x]
 
     per = parts * toks
-    resp_tile, prompt_tile = 2 * per, rows
+    resp_tile, prompt_tile = resp_rows, GROUP * rows
 
     def resp_slot(x, slot):
         attend(
@@ -204,12 +201,12 @@
 
     def prompt_slot(x, slot):
         def visible(shape):
-            row = lax.broadcasted_iota(jnp.int32, shape, 0) + y * rows
+            row = lax.rem(lax.broadcasted_iota(jnp.int32, shape, 0), rows) + y * rows
             return lax.broadcasted_iota(jnp.int32, shape, 1) <= row
 
         def run():
             attend(
-                x, block(kbuf, slot, x), block(vbuf, slot, x), resp_rows, prompt_tile, GROUP,
+                x, block(kbuf, slot, x), block(vbuf, slot, x), resp_rows, prompt_tile, 1,
                 slot == 0, visible if slot == 0 else None,
             )
 
@@ -283,15 +280,16 @@
             arrived(("q", x, d))
         stack_resp(x)
 
+    for copy in got_kv:
+        copy.wait()
     first_sends(0)
+    first_sends(1)
     swap_q(0)
     swap_kv()
-    first_sends(1)
     swap_q(1)
-
     got_pq.wait()
     stack_prompt()
-    for copy in got_kv + got_resp:
+    for copy in got_resp:
         copy.wait()
     y2(0, 0)
     y2(1, 0)
@@ -301,34 +299,34 @@
     whole(1, 0)
     prompt_slot(1, 0)
     after_z1(1)
-    y2(0, 1)
-    y2(0, 2)
     take_resp(0)
     resp_own(0)
     resp_slot(0, 0)
-    after_z2(0)
+    y2(0, 1)
+    y2(0, 2)
+    take_resp(1)
+    resp_own(1)
+    resp_slot(1, 0)
     y2(1, 1)
     y2(1, 2)
+    after_z2(0)
     whole(0, 1)
     resp_slot(0, 1)
-    prompt_slot(0, 1)
-    after_z2(1)
-    y2(0, 3)
     whole(0, 2)
     resp_slot(0, 2)
+    after_z2(1)
+    whole(1, 1)
+    resp_slot(1, 1)
+    whole(1, 2)
+    resp_slot(1, 2)
+    y2(0, 3)
+    prompt_slot(0, 1)
     prompt_slot(0, 2)
     y2(1, 3)
     whole(0, 3)
     resp_slot(0, 3)
     finish_resp(0)
     swap_out(0)
-    take_resp(1)
-    resp_own(1)
-    resp_slot(1, 0)
-    whole(1, 1)
-    resp_slot(1, 1)
-    whole(1, 2)
-    resp_slot(1, 2)
     whole(1, 3)
     resp_slot(1, 3)
     finish_resp(1)
@@ -344,7 +342,7 @@
             arrived(("o", x, d))
     for copy in sent.values():
         copy.wait_send()
-    for copy in local[6:]:
+    for copy in local[1 + len(got_kv) + len(got_resp):]:
         copy.wait()
 
 
@@ -355,7 +353,7 @@
     parts = lax.axis_size("head")
     kv = kwidth // HEAD_DIM
     total = GROUP * (rows + parts * toks)
-    any_place = pl.BlockSpec(memory_space=pl.ANY)
+    any_place = pl.BlockSpec(memory_space=pltpu.HBM)
     bf16 = jnp.bfloat16
     messages = 80
     prompt_out, mixed = pl.pallas_call(
@@ -367,8 +365,8 @@
         in_specs=[any_place] * 6,
         out_specs=(any_place, any_place),
         scratch_shapes=[
-            pltpu.VMEM((RING, RING * rows, kwidth), bf16),
-            pltpu.VMEM((RING, RING * rows, kwidth), bf16),
+            pltpu.VMEM((RING, kv, RING * rows, HEAD_DIM), bf16),
+            pltpu.VMEM((RING, kv, RING * rows, HEAD_DIM), bf16),
             pltpu.VMEM((rows, qwidth), bf16),
             pltpu.VMEM((parts, toks, qwidth), bf16),
             pltpu.VMEM((parts, toks, kwidth), bf16),

time: 77.1 us -> 61.4 us (0.80)
  the two profiles are of different devices: /device:TPU:418 before, /device:TPU:4 now
where the time goes in v2:
time: 61.4 us; the launch traced here: 61 us
  Pallas kernels  53 us (86%)
  local copies, waits for them, and re-layouts  5.88 us (10%)
  between operations  1.31 us (2%)
  other arithmetic  0.8 us (1%)
    pallas_call x1, Pallas kernels, on_device(): pl.pallas_call(functools.partial(kernel, (rows, toks, parts)), out_shape=...  53 us
    unnamed x13, local copies, waits for them, and re-layouts  5.88 us

profile of v2, /device:TPU:4, one launch (start us, length us, event | category | flops | bytes accessed | tf_op | source)
XLA Modules:
  0.0 61.0 jit_solution(16473558953641218957)
XLA Ops:
  0.6 0.0 copy-start
  0.6 1.0 %copy-done = bf16[112,2048]{1,0:T(8,128)(2,1)S(1)} copy-done((bf16[112,2048]{1,0:T(8,128)(2,1)S(1)}, bf16[112,2048]{1,0:T(8,128)(2,1)}, u32[]{:S(2)}) %copy-start) | copy-done | bytes 458776
  1.7 0.0 copy-start.1
  1.7 0.9 %copy-done.1 = bf16[1,16,8192]{2,1,0:T(8,128)(2,1)S(1)} copy-done((bf16[1,16,8192]{2,1,0:T(8,128)(2,1)S(1)}, bf16[1,16,8192]{2,1,0:T(8,128)(2,1)}, u32[]{:S(2)}) %copy-start.1) | copy-done | bytes 262168
  2.6 0.0 copy-start.2
  2.6 0.8 %copy-done.2 = bf16[112,256]{1,0:T(8,128)(2,1)S(1)} copy-done((bf16[112,256]{1,0:T(8,128)(2,1)S(1)}, bf16[112,256]{1,0:T(8,128)(2,1)}, u32[]{:S(2)}) %copy-start.2) | copy-done | bytes 57368
  3.4 0.0 copy-start.3
  3.4 0.8 %copy-done.3 = bf16[112,256]{1,0:T(8,128)(2,1)S(1)} copy-done((bf16[112,256]{1,0:T(8,128)(2,1)S(1)}, bf16[112,256]{1,0:T(8,128)(2,1)}, u32[]{:S(2)}) %copy-start.3) | copy-done | bytes 57368
  4.2 0.0 copy-start.4
  4.2 0.8 %copy-done.4 = bf16[1,16,1024]{2,1,0:T(8,128)(2,1)S(1)} copy-done((bf16[1,16,1024]{2,1,0:T(8,128)(2,1)S(1)}, bf16[1,16,1024]{2,1,0:T(8,128)(2,1)}, u32[]{:S(2)}) %copy-start.4) | copy-done | bytes 32792
  5.0 0.0 copy-start.5
  5.0 0.8 %copy-done.5 = bf16[1,16,1024]{2,1,0:T(8,128)(2,1)S(1)} copy-done((bf16[1,16,1024]{2,1,0:T(8,128)(2,1)S(1)}, bf16[1,16,1024]{2,1,0:T(8,128)(2,1)}, u32[]{:S(2)}) %copy-start.5) | copy-done | bytes 32792
  5.8 53.0 %shard_map.86 = (bf16[112,2048]{1,0:T(8,128)(2,1)S(1)}, bf16[16,8192]{1,0:T(8,128)(2,1)S(1)}) custom-call(bf16[112,2048]{1,0:T(8,128)(2,1)S(1)} %copy-done, bf16[112,256]{1,0:T(8,128)(2,1)S(1)} %copy-done.2, bf16[112,256]{1,0:T(8,128)(2,1)S(1)} %copy-done.3, bf16[16,8192]{1,0:T(8,128)(2,1)S(1)} %bitcast.7, bf16[16,1024]{1,0:T(8,128)(2,1)S(1)} %bitcast.8, ...), custom_call_target="tpu_custom_call" | custom-call | tf_op jit(solution)/shard_map/pallas_call | solution.py:359
  59.4 0.8 %select_bitcast_fusion = bf16[1,16,8192]{2,1,0:T(8,128)(2,1)} fusion(bf16[16,8192]{1,0:T(8,128)(2,1)S(1)} %get-tuple-element.5, pred[16]{0:T(512)(128)(4,1)S(1)} %add_compare_fusion), kind=kLoop, calls=%fused_computation | loop fusion | flops 131072 | bytes 524304 | tf_op jit(solution)/shard_map/broadcast_in_dim | solution.py:389
  60.2 0.8 %copy.11 = bf16[112,2048]{1,0:T(8,128)(2,1)} copy(bf16[112,2048]{1,0:T(8,128)(2,1)S(1)} %get-tuple-element.8) | data formatting | bytes 917504
  (1 shorter events, 0.0 us)
Async XLA Ops:
  0.6 1.0 %copy-start = (bf16[112,2048]{1,0:T(8,128)(2,1)S(1)}, bf16[112,2048]{1,0:T(8,128)(2,1)}, u32[]{:S(2)}) copy-start(bf16[112,2048]{1,0:T(8,128)(2,1)} %pq_ref.1) | copy-start | bytes 1376260
  1.7 0.9 %copy-start.1 = (bf16[1,16,8192]{2,1,0:T(8,128)(2,1)S(1)}, bf16[1,16,8192]{2,1,0:T(8,128)(2,1)}, u32[]{:S(2)}) copy-start(bf16[1,16,8192]{2,1,0:T(8,128)(2,1)} %param.10) | copy-start | bytes 786436
  2.6 0.8 %copy-start.2 = (bf16[112,256]{1,0:T(8,128)(2,1)S(1)}, bf16[112,256]{1,0:T(8,128)(2,1)}, u32[]{:S(2)}) copy-start(bf16[112,256]{1,0:T(8,128)(2,1)} %pk_ref.1) | copy-start | bytes 172036
  3.4 0.8 %copy-start.3 = (bf16[112,256]{1,0:T(8,128)(2,1)S(1)}, bf16[112,256]{1,0:T(8,128)(2,1)}, u32[]{:S(2)}) copy-start(bf16[112,256]{1,0:T(8,128)(2,1)} %pv_ref.1) | copy-start | bytes 172036
  4.2 0.8 %copy-start.4 = (bf16[1,16,1024]{2,1,0:T(8,128)(2,1)S(1)}, bf16[1,16,1024]{2,1,0:T(8,128)(2,1)}, u32[]{:S(2)}) copy-start(bf16[1,16,1024]{2,1,0:T(8,128)(2,1)} %param.11) | copy-start | bytes 98308
  5.0 0.8 %copy-start.5 = (bf16[1,16,1024]{2,1,0:T(8,128)(2,1)S(1)}, bf16[1,16,1024]{2,1,0:T(8,128)(2,1)}, u32[]{:S(2)}) copy-start(bf16[1,16,1024]{2,1,0:T(8,128)(2,1)} %param.12) | copy-start | bytes 98308

commit v3 on v2

--- a/solution.py
+++ b/solution.py
@@ -113,11 +113,11 @@
         for way in (1, -1) if a == "k" else (-1, 1):
             send(("y1", a, x, slot, way), place, place, {"seq": y_next if way > 0 else y_prev})
 
-    def y2(x, slot):
-        for a, way in (("k", 1), ("v", -1)):
-            arrived(("y1", a, x, slot, way))
-            place = bufs[a].at[slot, x, rows_of(-way)]
-            send(("y2", a, x, slot), place, place, {"seq": y_next if way > 0 else y_prev})
+    def y2(a, x, slot):
+        way = 1 if a == "k" else -1
+        arrived(("y1", a, x, slot, way))
+        place = bufs[a].at[slot, x, rows_of(-way)]
+        send(("y2", a, x, slot), place, place, {"seq": y_next if way > 0 else y_prev})
 
     def whole(x, slot):
         for a, way in (("k", -1), ("v", 1)):
@@ -246,25 +246,33 @@
         part = pl.ds(x * wide, wide)
         bring(pob.at[:, part], po_ref.at[:, part])
 
-    def first_sends(x):
-        z1("k", x, 1)
-        z1("v", x, -1)
-        z1("v", x, 1)
-        z1("k", x, -1)
-        y1("k", x, 0)
-        y1("v", x, 0)
-
-    def after_z1(x):
-        arrived(("z1", "k", x, 1))
-        z2("k", x)
-        y1("k", x, 1)
-        arrived(("z1", "v", x, -1))
-        z2("v", x)
-        y1("v", x, 2)
-        arrived(("z1", "v", x, 1))
-        y1("v", x, 1)
-        arrived(("z1", "k", x, -1))
-        y1("k", x, 2)
+    left = set()
+
+    def gone(name):
+        if name not in left:
+            left.add(name)
+            sent[name].wait_send()
+
+    def first_z(pairs):
+        for x in range(kv):
+            for a, way in pairs:
+                z1(a, x, way)
+
+    def first_y():
+        for x in range(kv):
+            y1("k", x, 0)
+            y1("v", x, 0)
+
+    def pass_on(x):
+        for a, slot, way in (("k", 1, 1), ("v", 2, -1)):
+            arrived(("z1", a, x, way))
+            z2(a, x)
+            y1(a, x, slot)
+
+    def spread(x):
+        for a, slot, way in (("v", 1, 1), ("k", 2, -1)):
+            arrived(("z1", a, x, way))
+            y1(a, x, slot)
 
     def after_z2(x):
         for a in "kv":
@@ -280,49 +288,61 @@
             arrived(("q", x, d))
         stack_resp(x)
 
+    onward = (("k", 1), ("v", -1))
+    rest = (("v", 1), ("k", -1))
     for copy in got_kv:
         copy.wait()
-    first_sends(0)
-    first_sends(1)
-    swap_q(0)
-    swap_kv()
-    swap_q(1)
+    first_z(onward)
+    first_y()
+    first_z(rest)
     got_pq.wait()
     stack_prompt()
     for copy in got_resp:
         copy.wait()
-    y2(0, 0)
-    y2(1, 0)
+    for x in range(kv):
+        y2("k", x, 0)
+        y2("v", x, 0)
+    pass_on(0)
     whole(0, 0)
     prompt_slot(0, 0)
-    after_z1(0)
+    pass_on(1)
     whole(1, 0)
+    swap_kv()
+    swap_q(0)
+    swap_q(1)
     prompt_slot(1, 0)
-    after_z1(1)
+    y2("k", 0, 1)
+    y2("v", 0, 2)
+    spread(0)
+    y2("k", 1, 1)
+    y2("v", 1, 2)
+    spread(1)
+    y2("v", 0, 1)
+    y2("k", 0, 2)
+    after_z2(0)
+    y2("v", 1, 1)
+    y2("k", 1, 2)
+    after_z2(1)
+    whole(0, 1)
+    prompt_slot(0, 1)
+    y2("k", 0, 3)
+    y2("v", 0, 3)
+    whole(0, 2)
+    prompt_slot(0, 2)
     take_resp(0)
     resp_own(0)
     resp_slot(0, 0)
-    y2(0, 1)
-    y2(0, 2)
+    y2("k", 1, 3)
+    y2("v", 1, 3)
+    resp_slot(0, 1)
+    resp_slot(0, 2)
     take_resp(1)
     resp_own(1)
     resp_slot(1, 0)
-    y2(1, 1)
-    y2(1, 2)
-    after_z2(0)
-    whole(0, 1)
-    resp_slot(0, 1)
-    whole(0, 2)
-    resp_slot(0, 2)
-    after_z2(1)
     whole(1, 1)
     resp_slot(1, 1)
     whole(1, 2)
     resp_slot(1, 2)
-    y2(0, 3)
-    prompt_slot(0, 1)
-    prompt_slot(0, 2)
-    y2(1, 3)
     whole(0, 3)
     resp_slot(0, 3)
     finish_resp(0)
@@ -340,8 +360,8 @@
     for x in range(kv):
         for d in range(parts - 1):
             arrived(("o", x, d))
-    for copy in sent.values():
-        copy.wait_send()
+    for name in sent:
+        gone(name)
     for copy in local[1 + len(got_kv) + len(got_resp):]:
         copy.wait()
 
@@ -359,8 +379,8 @@
     prompt_out, mixed = pl.pallas_call(
         functools.partial(kernel, (rows, toks, parts)),
         out_shape=(
-            jax.ShapeDtypeStruct((rows, qwidth), bf16),
-            jax.ShapeDtypeStruct((toks, parts * qwidth), bf16),
+            pltpu.VMEM((rows, qwidth), bf16),
+            pltpu.VMEM((toks, parts * qwidth), bf16),
         ),
         in_specs=[any_place] * 6,
         out_specs=(any_place, any_place),
@@ -381,7 +401,7 @@
             pltpu.SemaphoreType.DMA((16,)),
         ],
         compiler_params=pltpu.CompilerParams(
-            collective_id=0, has_side_effects=True, vmem_limit_bytes=48 * 1024 * 1024
+            collective_id=0, has_side_effects=True, vmem_limit_bytes=60 * 1024 * 1024
         ),
     )(prompt_q, prompt_k, prompt_v, resp_q[0], resp_k[0], resp_v[0])
     positions = lax.axis_index("head") * toks + jnp.arange(toks)

time: 61.4 us -> 51.1 us (0.83)
  the two profiles are of different devices: /device:TPU:4 before, /device:TPU:24 now
where the time goes in v3:
time: 51.1 us; the launch traced here: 50.2 us
  Pallas kernels  47.3 us (93%)
  between operations  1.3 us (3%)
  other arithmetic  0.8 us (2%)
  local copies, waits for them, and re-layouts  0.77 us (2%)
    pallas_call x1, Pallas kernels, on_device(): pl.pallas_call(functools.partial(kernel, (rows, toks, parts)), out_shape=...  47.3 us

profile of v3, /device:TPU:24, one launch (start us, length us, event | category | flops | bytes accessed | tf_op | source)
XLA Modules:
  0.0 50.2 jit_solution(14356589178883084830)
XLA Ops:
  0.6 47.3 %shard_map.86 = (bf16[112,2048]{1,0:T(8,128)(2,1)S(1)}, bf16[16,8192]{1,0:T(8,128)(2,1)S(1)}) custom-call(bf16[112,2048]{1,0:T(8,128)(2,1)} %pq_ref.1, bf16[112,256]{1,0:T(8,128)(2,1)} %pk_ref.1, bf16[112,256]{1,0:T(8,128)(2,1)} %pv_ref.1, bf16[16,8192]{1,0:T(8,128)(2,1)} %bitcast.7, bf16[16,1024]{1,0:T(8,128)(2,1)} %bitcast.8, bf16[16,1024]{1,0:T(8,128)(2,1)} %bitcast.9), custom_call_target="tpu_custom_call" | custom-call | tf_op jit(solution)/shard_map/pallas_call | solution.py:379
  47.9 0.8 %copy.10 = bf16[112,2048]{1,0:T(8,128)(2,1)} copy(bf16[112,2048]{1,0:T(8,128)(2,1)S(1)} %get-tuple-element.6) | data formatting | bytes 917504
  49.4 0.8 %select_bitcast_fusion = bf16[1,16,8192]{2,1,0:T(8,128)(2,1)} fusion(bf16[16,8192]{1,0:T(8,128)(2,1)S(1)} %get-tuple-element.5, pred[16]{0:T(512)(128)(4,1)S(1)} %add_compare_fusion), kind=kLoop, calls=%fused_computation | loop fusion | flops 131072 | bytes 524304 | tf_op jit(solution)/shard_map/broadcast_in_dim | solution.py:409
  (1 shorter events, 0.0 us)

commit v4 on v3

--- a/solution.py
+++ b/solution.py
@@ -43,7 +43,7 @@
     others = [lax.rem(head + d, parts) for d in range(1, parts)]
 
     barrier = pltpu.get_barrier_semaphore()
-    for peer in (z_next, z_prev, y_next, y_prev):
+    for peer in (z_next, z_prev, y_next, y_prev, at(0, 2)):
         pl.semaphore_signal(barrier, inc=1, device_id={"seq": peer}, device_id_type=MESH)
     for peer in others:
         pl.semaphore_signal(barrier, inc=1, device_id={"head": peer}, device_id_type=MESH)
@@ -75,8 +75,9 @@
         bring(rk_ref.at[:, own_kv], rkb.at[head]),
         bring(rv_ref.at[:, own_kv], rvb.at[head]),
     ]
-    pl.semaphore_wait(barrier, 4 + len(others))
-
+    pl.semaphore_wait(barrier, 5 + len(others))
+
+    straight = (0, 1, 2, 3)
     sent = {}
 
     def send(name, src, dst, peer):
@@ -110,10 +111,13 @@
 
     def y1(a, x, slot):
         place = bufs[a].at[slot, x, mine]
-        for way in (1, -1) if a == "k" else (-1, 1):
-            send(("y1", a, x, slot, way), place, place, {"seq": y_next if way > 0 else y_prev})
+        ways = (1, -1) if a == "k" else (-1, 1)
+        for way in ways + ((2,) if slot in straight else ()):
+            send(("y1", a, x, slot, way), place, place, {"seq": at(0, way)})
 
     def y2(a, x, slot):
+        if slot in straight:
+            return
         way = 1 if a == "k" else -1
         arrived(("y1", a, x, slot, way))
         place = bufs[a].at[slot, x, rows_of(-way)]
@@ -121,9 +125,10 @@
 
     def whole(x, slot):
         for a, way in (("k", -1), ("v", 1)):
+            if slot in straight:
+                arrived(("y1", a, x, slot, -way))
             arrived(("y1", a, x, slot, way))
-        for a in "kv":
-            arrived(("y2", a, x, slot))
+            arrived(("y1", a, x, slot, 2) if slot in straight else ("y2", a, x, slot))
 
     def swap_q(x):
         for d, peer in enumerate(others):
@@ -375,7 +380,7 @@
     total = GROUP * (rows + parts * toks)
     any_place = pl.BlockSpec(memory_space=pltpu.HBM)
     bf16 = jnp.bfloat16
-    messages = 80
+    messages = 88
     prompt_out, mixed = pl.pallas_call(
         functools.partial(kernel, (rows, toks, parts)),
         out_shape=(

time: 51.1 us -> 49.2 us (0.963); the launches traced: 50.2 us -> 49 us
  Pallas kernels: 47.3 us -> 46.2 us
    pallas_call x1, Pallas kernels: 47.3 us -> 46.2 us  [on_device(): pl.pallas_call(functools.partial(kernel, (rows, toks, parts)), out_shape=...]
where the time goes in v4:
time: 49.2 us; the launch traced here: 49 us
  Pallas kernels  46.2 us (94%)
  between operations  1.3 us (3%)
  other arithmetic  0.8 us (2%)
  local copies, waits for them, and re-layouts  0.77 us (2%)
    pallas_call x1, Pallas kernels, on_device(): pl.pallas_call(functools.partial(kernel, (rows, toks, parts)), out_shape=...  46.2 us

profile of v4, /device:TPU:24, one launch (start us, length us, event | category | flops | bytes accessed | tf_op | source)
XLA Modules:
  0.0 49.0 jit_solution(15627413664396965015)
XLA Ops:
  0.6 46.2 %shard_map.86 = (bf16[112,2048]{1,0:T(8,128)(2,1)S(1)}, bf16[16,8192]{1,0:T(8,128)(2,1)S(1)}) custom-call(bf16[112,2048]{1,0:T(8,128)(2,1)} %pq_ref.1, bf16[112,256]{1,0:T(8,128)(2,1)} %pk_ref.1, bf16[112,256]{1,0:T(8,128)(2,1)} %pv_ref.1, bf16[16,8192]{1,0:T(8,128)(2,1)} %bitcast.7, bf16[16,1024]{1,0:T(8,128)(2,1)} %bitcast.8, bf16[16,1024]{1,0:T(8,128)(2,1)} %bitcast.9), custom_call_target="tpu_custom_call" | custom-call | tf_op jit(solution)/shard_map/pallas_call | solution.py:384
  46.8 0.8 %copy.10 = bf16[112,2048]{1,0:T(8,128)(2,1)} copy(bf16[112,2048]{1,0:T(8,128)(2,1)S(1)} %get-tuple-element.6) | data formatting | bytes 917504
  48.2 0.8 %select_bitcast_fusion = bf16[1,16,8192]{2,1,0:T(8,128)(2,1)} fusion(bf16[16,8192]{1,0:T(8,128)(2,1)S(1)} %get-tuple-element.5, pred[16]{0:T(512)(128)(4,1)S(1)} %add_compare_fusion), kind=kLoop, calls=%fused_computation | loop fusion | flops 131072 | bytes 524304 | tf_op jit(solution)/shard_map/broadcast_in_dim | solution.py:414
  (1 shorter events, 0.0 us)

commit v5 on v2

--- a/solution.py
+++ b/solution.py
@@ -42,8 +42,10 @@
     y_next, y_prev = at(0, 1), at(0, -1)
     others = [lax.rem(head + d, parts) for d in range(1, parts)]
 
+    along_z = {1: z_next, -1: z_prev}
+
     barrier = pltpu.get_barrier_semaphore()
-    for peer in (z_next, z_prev, y_next, y_prev):
+    for peer in (z_next, z_prev, y_next, y_prev, at(0, 2)):
         pl.semaphore_signal(barrier, inc=1, device_id={"seq": peer}, device_id_type=MESH)
     for peer in others:
         pl.semaphore_signal(barrier, inc=1, device_id={"head": peer}, device_id_type=MESH)
@@ -75,80 +77,78 @@
         bring(rk_ref.at[:, own_kv], rkb.at[head]),
         bring(rv_ref.at[:, own_kv], rvb.at[head]),
     ]
-    pl.semaphore_wait(barrier, 4 + len(others))
-
-    sent = {}
-
-    def send(name, src, dst, peer):
-        copy = pltpu.make_async_remote_copy(
+    pl.semaphore_wait(barrier, 5 + len(others))
+
+    number = {}
+
+    def message(name):
+        kind, *which = name
+        if kind == "z1":
+            a, x, way = which
+            src, dst = bufs[a].at[0, x, mine], bufs[a].at[1 if way > 0 else 2, x, mine]
+            peer = {"seq": along_z[way]}
+        elif kind == "z2":
+            a, x = which
+            slot, way = (1, 1) if a == "k" else (2, -1)
+            src, dst = bufs[a].at[slot, x, mine], bufs[a].at[3, x, mine]
+            peer = {"seq": along_z[way]}
+        elif kind == "y":
+            a, x, slot, way = which
+            src = dst = bufs[a].at[slot, x, mine]
+            peer = {"seq": at(0, way)}
+        else:
+            *x, d = which
+            peer = {"head": others[d]}
+            if kind == "q":
+                begin = pl.multiple_of(others[d] * qwidth + x[0] * wide, wide)
+                src = rq_ref.at[:, pl.ds(begin, wide)]
+                dst = rqb.at[head, :, pl.ds(x[0] * wide, wide)]
+            elif kind == "o":
+                to = pl.multiple_of(head * qwidth + x[0] * wide, wide)
+                src = rob.at[others[d], :, pl.ds(x[0] * wide, wide)]
+                dst = ro_ref.at[:, pl.ds(to, wide)]
+            else:
+                begin = pl.multiple_of(others[d] * kv * HEAD_DIM, kv * HEAD_DIM)
+                given, held = (rk_ref, rkb) if kind == "rk" else (rv_ref, rvb)
+                src, dst = given.at[:, pl.ds(begin, kv * HEAD_DIM)], held.at[head]
+        at_sem = number.setdefault(name, len(number))
+        return pltpu.make_async_remote_copy(
             src_ref=src,
             dst_ref=dst,
-            send_sem=send_sem.at[len(sent)],
-            recv_sem=recv_sem.at[len(sent)],
+            send_sem=send_sem.at[at_sem],
+            recv_sem=recv_sem.at[at_sem],
             device_id=peer,
             device_id_type=MESH,
         )
-        copy.start()
-        sent[name] = copy
-
-    def arrived(name):
-        sent[name].wait_recv()
-
-    def z1(a, x, way):
-        slot = 1 if way > 0 else 2
-        send(
-            ("z1", a, x, way), bufs[a].at[0, x, mine], bufs[a].at[slot, x, mine],
-            {"seq": z_next if way > 0 else z_prev},
-        )
-
-    def z2(a, x):
-        slot, peer = (1, z_next) if a == "k" else (2, z_prev)
-        send(
-            ("z2", a, x), bufs[a].at[slot, x, mine], bufs[a].at[3, x, mine],
-            {"seq": peer},
-        )
+
+    def send(*name):
+        message(name).start()
+
+    def arrived(*name):
+        message(name).wait_recv()
 
     def y1(a, x, slot):
-        place = bufs[a].at[slot, x, mine]
-        for way in (1, -1) if a == "k" else (-1, 1):
-            send(("y1", a, x, slot, way), place, place, {"seq": y_next if way > 0 else y_prev})
-
-    def y2(x, slot):
-        for a, way in (("k", 1), ("v", -1)):
-            arrived(("y1", a, x, slot, way))
-            place = bufs[a].at[slot, x, rows_of(-way)]
-            send(("y2", a, x, slot), place, place, {"seq": y_next if way > 0 else y_prev})
+        for way in (1, -1, 2) if a == "k" else (-1, 1, 2):
+            send("y", a, x, slot, way)
 
     def whole(x, slot):
-        for a, way in (("k", -1), ("v", 1)):
-            arrived(("y1", a, x, slot, way))
-        for a in "kv":
-            arrived(("y2", a, x, slot))
+        for way in (1, -1, 2):
+            for a in "kv":
+                arrived("y", a, x, slot, way)
 
     def swap_q(x):
-        for d, peer in enumerate(others):
-            begin = pl.multiple_of(peer * qwidth + x * wide, wide)
-            send(
-                ("q", x, d), rq_ref.at[:, pl.ds(begin, wide)],
-                rqb.at[head, :, pl.ds(x * wide, wide)], {"head": peer},
-            )
+        for d in range(parts - 1):
+            send("q", x, d)
 
     def swap_kv():
-        for d, peer in enumerate(others):
-            begin = pl.multiple_of(peer * kv * HEAD_DIM, kv * HEAD_DIM)
-            for name, src, dst in (("rk", rk_ref, rkb), ("rv", rv_ref, rvb)):
-                send(
-                    (name, d), src.at[:, pl.ds(begin, kv * HEAD_DIM)], dst.at[head],
-                    {"head": peer},
-                )
+        for d in range(parts - 1):
+            send("rk", d)
+            send("rv", d)
 
     def swap_out(x):
+        for d in range(parts - 1):
+            send("o", x, d)
         to = pl.multiple_of(head * qwidth + x * wide, wide)
-        for d, peer in enumerate(others):
-            send(
-                ("o", x, d), rob.at[peer, :, pl.ds(x * wide, wide)],
-                ro_ref.at[:, pl.ds(to, wide)], {"head": peer},
-            )
         bring(rob.at[head, :, pl.ds(x * wide, wide)], ro_ref.at[:, pl.ds(to, wide)])
 
     def attend(x, keys, values, begin, tile, count, first, visible):
@@ -189,6 +189,14 @@
             False, None,
         )
 
+    def resp_middle(x):
+        def both(buf):
+            return lambda: buf[1:3, x].reshape(2 * chunk, HEAD_DIM)
+
+        attend(
+            x, both(kbuf), both(vbuf), 0, resp_tile, resp_rows // resp_tile, False, None,
+        )
+
     def resp_own(x):
         def flat(buf):
             return lambda: buf[:, :, x * HEAD_DIM : (x + 1) * HEAD_DIM].reshape(per, HEAD_DIM)
@@ -246,104 +254,105 @@
         part = pl.ds(x * wide, wide)
         bring(pob.at[:, part], po_ref.at[:, part])
 
-    def first_sends(x):
-        z1("k", x, 1)
-        z1("v", x, -1)
-        z1("v", x, 1)
-        z1("k", x, -1)
-        y1("k", x, 0)
-        y1("v", x, 0)
-
-    def after_z1(x):
-        arrived(("z1", "k", x, 1))
-        z2("k", x)
-        y1("k", x, 1)
-        arrived(("z1", "v", x, -1))
-        z2("v", x)
-        y1("v", x, 2)
-        arrived(("z1", "v", x, 1))
-        y1("v", x, 1)
-        arrived(("z1", "k", x, -1))
-        y1("k", x, 2)
+    order = {1: "kv", -1: "vk"}
+
+    def spread(a, x, way):
+        arrived("z1", a, x, way)
+        y1(a, x, 1 if way > 0 else 2)
+
+    def pass_on(a, x, way):
+        arrived("z1", a, x, way)
+        send("z2", a, x)
+        y1(a, x, 1 if way > 0 else 2)
 
     def after_z2(x):
         for a in "kv":
-            arrived(("z2", a, x))
+            arrived("z2", a, x)
             y1(a, x, 3)
 
     def take_resp(x):
         if x == 0:
             for d in range(parts - 1):
-                arrived(("rk", d))
-                arrived(("rv", d))
+                arrived("rk", d)
+                arrived("rv", d)
         for d in range(parts - 1):
-            arrived(("q", x, d))
+            arrived("q", x, d)
         stack_resp(x)
 
     for copy in got_kv:
         copy.wait()
-    first_sends(0)
-    first_sends(1)
-    swap_q(0)
-    swap_kv()
-    swap_q(1)
+
+    def first_z(position):
+        for x in range(kv):
+            for way in (1, -1):
+                send("z1", order[way][position], x, way)
+
+    first_z(0)
+    for x in range(kv):
+        for a in "kv":
+            y1(a, x, 0)
+    first_z(1)
     got_pq.wait()
     stack_prompt()
     for copy in got_resp:
         copy.wait()
-    y2(0, 0)
-    y2(1, 0)
+    pass_on("k", 0, 1)
+    pass_on("v", 0, -1)
     whole(0, 0)
-    prompt_slot(0, 0)
-    after_z1(0)
+    pl.when(zh != 0)(lambda: prompt_slot(0, 0))
+    pass_on("k", 1, 1)
+    pass_on("v", 1, -1)
+    swap_q(0)
+    swap_kv()
+    swap_q(1)
     whole(1, 0)
-    prompt_slot(1, 0)
-    after_z1(1)
-    take_resp(0)
-    resp_own(0)
-    resp_slot(0, 0)
-    y2(0, 1)
-    y2(0, 2)
-    take_resp(1)
-    resp_own(1)
-    resp_slot(1, 0)
-    y2(1, 1)
-    y2(1, 2)
+    pl.when(zh != 0)(lambda: prompt_slot(1, 0))
+    for x in range(kv):
+        spread("v", x, 1)
+        spread("k", x, -1)
     after_z2(0)
-    whole(0, 1)
-    resp_slot(0, 1)
-    whole(0, 2)
-    resp_slot(0, 2)
     after_z2(1)
-    whole(1, 1)
-    resp_slot(1, 1)
-    whole(1, 2)
-    resp_slot(1, 2)
-    y2(0, 3)
-    prompt_slot(0, 1)
-    prompt_slot(0, 2)
-    y2(1, 3)
-    whole(0, 3)
-    resp_slot(0, 3)
-    finish_resp(0)
-    swap_out(0)
-    whole(1, 3)
-    resp_slot(1, 3)
-    finish_resp(1)
-    swap_out(1)
-    prompt_slot(0, 3)
-    finish_prompt(0)
-    prompt_slot(1, 1)
-    prompt_slot(1, 2)
-    prompt_slot(1, 3)
-    finish_prompt(1)
+    for x in range(kv):
+        take_resp(x)
+        resp_own(x)
+        resp_slot(x, 0)
+        whole(x, 1)
+        whole(x, 2)
+        resp_middle(x)
+    for x in range(kv):
+        whole(x, 3)
+        resp_slot(x, 3)
+        finish_resp(x)
+        swap_out(x)
+    for x in range(kv):
+        pl.when(zh == 0)(lambda x=x: prompt_slot(x, 0))
+        for slot in range(1, RING):
+            prompt_slot(x, slot)
+        finish_prompt(x)
     for x in range(kv):
         for d in range(parts - 1):
-            arrived(("o", x, d))
-    for copy in sent.values():
-        copy.wait_send()
+            arrived("o", x, d)
+    for name in number:
+        message(name).wait_send()
     for copy in local[1 + len(got_kv) + len(got_resp):]:
         copy.wait()
+
+
+def hand_over(toks, lengths_ref, prompt_ref, mixed_ref, prompt_out_ref, resp_out_ref, held, sems):
+    copies = [
+        pltpu.make_async_copy(prompt_ref, prompt_out_ref, sems.at[0]),
+        pltpu.make_async_copy(mixed_ref, held, sems.at[1]),
+        pltpu.make_async_copy(held, resp_out_ref, sems.at[2]),
+    ]
+    copies[1].start()
+    copies[0].start()
+    copies[1].wait()
+    position = lax.axis_index("head") * toks + lax.broadcasted_iota(jnp.int32, held.shape, 0)
+    mixed = held[...]
+    held[...] = jnp.where(position < lengths_ref[0], mixed, jnp.zeros_like(mixed))
+    copies[2].start()
+    copies[0].wait()
+    copies[2].wait()
 
 
 def on_device(prompt_q, prompt_k, prompt_v, resp_q, resp_k, resp_v, lengths):
@@ -355,12 +364,13 @@
     total = GROUP * (rows + parts * toks)
     any_place = pl.BlockSpec(memory_space=pltpu.HBM)
     bf16 = jnp.bfloat16
-    messages = 80
-    prompt_out, mixed = pl.pallas_call(
+    messages = 88
+    plain = pl.BlockSpec(memory_space=pl.ANY)
+    prompt_raw, mixed = pl.pallas_call(
         functools.partial(kernel, (rows, toks, parts)),
         out_shape=(
-            jax.ShapeDtypeStruct((rows, qwidth), bf16),
-            jax.ShapeDtypeStruct((toks, parts * qwidth), bf16),
+            pltpu.VMEM((rows, qwidth), bf16),
+            pltpu.VMEM((toks, parts * qwidth), bf16),
         ),
         in_specs=[any_place] * 6,
         out_specs=(any_place, any_place),
@@ -381,13 +391,27 @@
             pltpu.SemaphoreType.DMA((16,)),
         ],
         compiler_params=pltpu.CompilerParams(
-            collective_id=0, has_side_effects=True, vmem_limit_bytes=48 * 1024 * 1024
+            collective_id=0, has_side_effects=True, vmem_limit_bytes=60 * 1024 * 1024
         ),
     )(prompt_q, prompt_k, prompt_v, resp_q[0], resp_k[0], resp_v[0])
-    positions = lax.axis_index("head") * toks + jnp.arange(toks)
-    live = positions < lengths[0]
-    resp_out = jnp.where(live[:, None], mixed, jnp.zeros_like(mixed))[None]
-    return (prompt_out, resp_out)
+    prompt_out, resp_out = pl.pallas_call(
+        functools.partial(hand_over, toks),
+        out_shape=(
+            jax.ShapeDtypeStruct((rows, qwidth), bf16),
+            jax.ShapeDtypeStruct((toks, parts * qwidth), bf16),
+        ),
+        in_specs=[pl.BlockSpec(memory_space=pltpu.SMEM), plain, plain],
+        out_specs=(plain, plain),
+        scratch_shapes=[
+            pltpu.VMEM((toks, parts * qwidth), bf16),
+            pltpu.SemaphoreType.DMA((3,)),
+        ],
+    )(
+        lengths,
+        pltpu.with_memory_space_constraint(prompt_raw, pltpu.VMEM),
+        pltpu.with_memory_space_constraint(mixed, pltpu.VMEM),
+    )
+    return (prompt_out, resp_out[None])
 
 
 def solution(mesh):

time: 61.4 us -> 48.7 us (0.79)
  the two profiles are of different devices: /device:TPU:4 before, /device:TPU:24 now
where the time goes in v5:
time: 48.7 us; the launch traced here: 48.6 us
  Pallas kernels  47.2 us (97%)
  between operations  1.45 us (3%)
    pallas_call x1, Pallas kernels, on_device(): pl.pallas_call(functools.partial(kernel, (rows, toks, parts)), out_shape=...  46.3 us

profile of v5, /device:TPU:24, one launch (start us, length us, event | category | flops | bytes accessed | tf_op | source)
XLA Modules:
  0.0 48.6 jit_solution(4037031669697199533)
XLA Ops:
  1.3 46.3 %shard_map.86 = (bf16[112,2048]{1,0:T(8,128)(2,1)S(1)}, bf16[16,8192]{1,0:T(8,128)(2,1)S(1)}) custom-call(bf16[112,2048]{1,0:T(8,128)(2,1)} %pq_ref.1, bf16[112,256]{1,0:T(8,128)(2,1)} %pk_ref.1, bf16[112,256]{1,0:T(8,128)(2,1)} %pv_ref.1, bf16[16,8192]{1,0:T(8,128)(2,1)} %bitcast.4, bf16[16,1024]{1,0:T(8,128)(2,1)} %bitcast.5, bf16[16,1024]{1,0:T(8,128)(2,1)} %bitcast.6), custom_call_target="tpu_custom_call" | custom-call | tf_op jit(solution)/shard_map/pallas_call | solution.py:369
  47.6 0.9 %shard_map.87 = (bf16[112,2048]{1,0:T(8,128)(2,1)}, bf16[16,8192]{1,0:T(8,128)(2,1)}) custom-call(s32[1]{0:T(128)S(6)} %copy.9.lengths_ref, bf16[112,2048]{1,0:T(8,128)(2,1)S(1)} %get-tuple-element.6.prompt_ref, bf16[16,8192]{1,0:T(8,128)(2,1)S(1)} %get-tuple-element.7.mixed_ref), custom_call_target="tpu_custom_call" | custom-call | tf_op jit(solution)/shard_map/pallas_call | solution.py:397

commit v6 on v5

--- a/solution.py
+++ b/solution.py
@@ -197,15 +197,21 @@
             x, both(kbuf), both(vbuf), 0, resp_tile, resp_rows // resp_tile, False, None,
         )
 
-    def resp_own(x):
-        def flat(buf):
-            return lambda: buf[:, :, x * HEAD_DIM : (x + 1) * HEAD_DIM].reshape(per, HEAD_DIM)
+    def resp_first(x):
+        def joined(buf, own):
+            return lambda: jnp.concatenate(
+                [buf[0, x], own[:, :, x * HEAD_DIM : (x + 1) * HEAD_DIM].reshape(per, HEAD_DIM)],
+                axis=0,
+            )
 
         def visible(shape):
             row = lax.rem(lax.broadcasted_iota(jnp.int32, shape, 0), per)
-            return lax.broadcasted_iota(jnp.int32, shape, 1) <= row
-
-        attend(x, flat(rkb), flat(rvb), 0, resp_tile, resp_rows // resp_tile, True, visible)
+            return lax.broadcasted_iota(jnp.int32, shape, 1) - chunk <= row
+
+        attend(
+            x, joined(kbuf, rkb), joined(vbuf, rvb), 0, resp_tile, resp_rows // resp_tile, True,
+            visible,
+        )
 
     def prompt_slot(x, slot):
         def visible(shape):
@@ -314,8 +320,7 @@
     after_z2(1)
     for x in range(kv):
         take_resp(x)
-        resp_own(x)
-        resp_slot(x, 0)
+        resp_first(x)
         whole(x, 1)
         whole(x, 2)
         resp_middle(x)

time: 48.7 us -> 48.1 us (0.988)
  Pallas kernels: 47.2 us -> 46.5 us
    pallas_call x1, Pallas kernels: 46.3 us -> 45.6 us  [on_device(): pl.pallas_call(functools.partial(kernel, (rows, toks, parts)), out_shape=...]
where the time goes in v6:
time: 48.1 us; the launch traced here: 48 us
  Pallas kernels  46.5 us (97%)
  between operations  1.45 us (3%)
    pallas_call x1, Pallas kernels, on_device(): pl.pallas_call(functools.partial(kernel, (rows, toks, parts)), out_shape=...  45.6 us

profile of v6, /device:TPU:24, one launch (start us, length us, event | category | flops | bytes accessed | tf_op | source)
XLA Modules:
  0.0 48.0 jit_solution(935320233291072500)
XLA Ops:
  1.3 45.6 %shard_map.86 = (bf16[112,2048]{1,0:T(8,128)(2,1)S(1)}, bf16[16,8192]{1,0:T(8,128)(2,1)S(1)}) custom-call(bf16[112,2048]{1,0:T(8,128)(2,1)} %pq_ref.1, bf16[112,256]{1,0:T(8,128)(2,1)} %pk_ref.1, bf16[112,256]{1,0:T(8,128)(2,1)} %pv_ref.1, bf16[16,8192]{1,0:T(8,128)(2,1)} %bitcast.4, bf16[16,1024]{1,0:T(8,128)(2,1)} %bitcast.5, bf16[16,1024]{1,0:T(8,128)(2,1)} %bitcast.6), custom_call_target="tpu_custom_call" | custom-call | tf_op jit(solution)/shard_map/pallas_call | solution.py:374
  46.9 0.9 %shard_map.87 = (bf16[112,2048]{1,0:T(8,128)(2,1)}, bf16[16,8192]{1,0:T(8,128)(2,1)}) custom-call(s32[1]{0:T(128)S(6)} %copy.9.lengths_ref, bf16[112,2048]{1,0:T(8,128)(2,1)S(1)} %get-tuple-element.6.prompt_ref, bf16[16,8192]{1,0:T(8,128)(2,1)S(1)} %get-tuple-element.7.mixed_ref), custom_call_target="tpu_custom_call" | custom-call | tf_op jit(solution)/shard_map/pallas_call | solution.py:402
